TPU v7x, 32 devices: a whole 2x2x4 slice. The times are simulated.
32 devices in a mesh: pole: 4 (over y, x), row: 2 (over core), col: 4 (over z).
Axes of the slice: x: 2, y: 2, z: 4, core: 2. Of those that a mesh axis runs over, the one named last changes fastest.
Arguments:
- hamiltonian_panel: bfloat16 [6144, 512], P(('row', 'col'), 'pole'), may hold values from -0.005859375 to 0.005859375
- margin_panel: bfloat16 [6144, 512], P(('row', 'col'), 'pole'), may hold values from -0.0029296875 to 0.0029296875
- shifts: float32 [4, 2], P('pole'), may hold values from -2 to 2
- weights: float32 [4, 2], P('pole'), may hold values from 0.5 to 2
- pivot_inverse: float32 [4, 2, 512, 512], P('pole'), may hold values from -6 to 6
- selected_inverse: bfloat16 [4, 2, 6144, 6144], P('pole', None, 'row', 'col'), may hold values from -6 to 6
Outputs:
- inverse_column: float32 [4, 6144, 2, 512], P('pole', ('row', 'col'))
- inverse_pivot: float32 [4, 2, 512, 512], P('pole')
- density_column: float32 [6144, 512], P(('row', 'col'), 'pole')
- density_pivot: float32 [512, 512], P('pole')
All inputs are finite; a program needn't handle non-finite values.
Results may differ from a plain program's by a relative error of at most 0.0037.
Values may be sent and summed in bfloat16 or wider, within the bound.
A program may use at most 128 MiB of HBM per device.

v0:
```python
import jax
import jax.numpy as jnp
from jax import lax
from jax.sharding import PartitionSpec as P

HALVES = 2


def precise(left, right):
    return jnp.dot(left, right, precision=lax.Precision.HIGH, preferred_element_type=jnp.float32)


def gather_panel(pair):
    return lax.all_gather(pair, "pole", axis=2, tiled=True)


def factor_panel(pair, shift, inverse):
    hamiltonian_f = pair[0].astype(jnp.float32)
    margin_f = pair[1].astype(jnp.float32)
    real_part = hamiltonian_f - shift[0] * margin_f
    imag_part = -shift[1] * margin_f
    lower_real = precise(real_part, inverse[0]) - precise(imag_part, inverse[1])
    lower_imag = precise(real_part, inverse[1]) + precise(imag_part, inverse[0])
    return (lower_real.astype(jnp.bfloat16), lower_imag.astype(jnp.bfloat16))


def half_dot(left, right):
    return lax.dot_general(
        left, right, (((0,), (0,)), ((), ())), preferred_element_type=jnp.float32
    )


def body(hamiltonian_panel, margin_panel, shifts, weights, pivot_inverse, selected_inverse):
    shift = shifts[0]
    weight = weights[0]
    inverse = pivot_inverse[0]
    block_real = selected_inverse[0, 0]
    block_imag = selected_inverse[0, 1]
    n_row = lax.axis_size("row")
    n_col = lax.axis_size("col")
    n_pole = lax.axis_size("pole")
    width = inverse.shape[-1]
    part = width // HALVES
    own_pair = jnp.stack([hamiltonian_panel, margin_panel])
    order = [(n_row * c + r, r * n_col + c) for r in range(n_row) for c in range(n_col)]
    met_pair = gather_panel(lax.ppermute(own_pair, ("row", "col"), order))
    met_real, met_imag = factor_panel(met_pair, shift, inverse)
    partials = []
    for h in range(HALVES):
        cut = slice(h * part, (h + 1) * part)
        mine = jnp.concatenate([met_real[:, cut], met_imag[:, cut]], axis=1)
        rows = lax.all_gather(mine, "row", axis=0, tiled=True)
        turned = jnp.concatenate([rows[:, part:], -rows[:, :part]], axis=1)
        total = jnp.dot(block_imag, turned, preferred_element_type=jnp.float32) - jnp.dot(
            block_real, rows, preferred_element_type=jnp.float32
        )
        partials.append(total.astype(jnp.bfloat16))
    own_pair, partials[-1] = lax.optimization_barrier((own_pair, partials[-1]))
    own_real, own_imag = factor_panel(gather_panel(own_pair), shift, inverse)
    lower = jnp.concatenate([own_real, own_imag], axis=1)
    columns = []
    updates = []
    for h in range(HALVES):
        column = lax.psum_scatter(partials[h], "col", scatter_dimension=0, tiled=True).astype(
            jnp.float32
        )
        high = column.astype(jnp.bfloat16)
        low = (column - high.astype(jnp.float32)).astype(jnp.bfloat16)
        square = half_dot(lower, high) + half_dot(lower, low)
        update = jnp.stack(
            [
                square[:width, :part] - square[width:, part:],
                square[:width, part:] + square[width:, :part],
            ]
        )
        updates.append(lax.psum(update, ("row", "col")))
        columns.append(column.reshape(column.shape[0], 2, part))
    column = jnp.concatenate(columns, axis=2)
    pivot = inverse - jnp.concatenate(updates, axis=2)
    column_density = weight[0] * column[:, 0] - weight[1] * column[:, 1]
    share = width // n_pole
    pieces = column_density.reshape(-1, n_pole, share).swapaxes(0, 1).astype(jnp.bfloat16)
    column_share = jnp.sum(
        lax.all_to_all(pieces, "pole", 0, 0, tiled=True).astype(jnp.float32), axis=0
    )
    pivot_density = weight[0] * pivot[0] - weight[1] * pivot[1]
    pieces = pivot_density.reshape(n_pole, share, width).astype(jnp.bfloat16)
    pivot_share = jnp.sum(
        lax.all_to_all(pieces, "pole", 0, 0, tiled=True).astype(jnp.float32), axis=0
    )
    return (column[None], pivot[None], column_share, pivot_share)


def solution(mesh):
    return jax.shard_map(
        body,
        mesh=mesh,
        in_specs=(
            P(("row", "col"), "pole"),
            P(("row", "col"), "pole"),
            P("pole", None),
            P("pole", None),
            P("pole", None, None, None),
            P("pole", None, "row", "col"),
        ),
        out_specs=(
            P("pole", ("row", "col"), None, None),
            P("pole", None, None, None),
            P(("row", "col"), "pole"),
            P("pole", None),
        ),
        check_vma=False,
    )
```

profile of v0, /device:TPU:0, one launch (start us, length us, event | category | flops | bytes accessed | tf_op | source)
XLA Modules:
  0.0 350.2 jit_solution(6100513097827890616)
XLA Ops:
  7.2 1.1 pad_maximum_fusion.6
  8.3 0.7 collective-permute-start
  9.0 0.7 copy-done.17
  9.8 1.3 fusion.112
  11.8 42.8 %all-gather.5.cloned.1.call-done = bf16[2,768,512]{2,1,0:T(8,128)(2,1)} async-done(((bf16[2,768,128]{2,1,0:T(8,128)(2,1)}), bf16[2,768,512]{2,1,0:T(8,128)(2,1)}) %all-gather.5.cloned.1.call-update) | async-done | bytes 1572880 | tf_op jit(solution)/shard_map/all_gather | solution.py:14
  54.6 3.2 fusion.28
  57.9 2.9 fusion.26
  60.7 2.3 subtract_convert_fusion.5
  63.0 2.3 add_convert_fusion.1
  65.4 0.9 pad_maximum_fusion.5
  66.4 1.0 pad_maximum_fusion.4
  67.5 8.9 %all-gather.9.cloned.1.call-done = bf16[1536,512]{0,1:T(8,128)(2,1)} async-done(((bf16[768,512]{0,1:T(8,128)(2,1)}), bf16[1536,512]{0,1:T(8,128)(2,1)}) %all-gather.9.cloned.1.call-update) | async-done | bytes 1572880 | tf_op jit(solution)/shard_map/all_gather | solution.py:52
  76.3 9.2 %fusion = f32[512,3072]{1,0:T(8,128)S(1)} fusion(bf16[1536,512]{0,1:T(8,128)(2,1)} %all-gather.9.cloned.1.call-done, bf16[1,2,3072,1536]{3,2,1,0:T(8,128)(2,1)} %param.11), kind=kOutput, calls=%fused_computation | convolution fusion | flops 4831838208 | bytes 17301504 | tf_op jit(solution)/shard_map/dot_general | solution.py:54
  85.7 11.0 %fusion.19 = bf16[3072,512]{0,1:T(8,128)(2,1)} fusion(f32[512,3072]{1,0:T(8,128)S(1)} %fusion, bf16[1,2,3072,1536]{3,2,1,0:T(8,128)(2,1)} %param.11, bf16[1536,256]{0,1:T(8,128)(2,1)S(1)} %get-tuple-element.25, bf16[1536,256]{0,1:T(8,128)(2,1)S(1)} %get-tuple-element.24), kind=kOutput, calls=%fused_computation.20 | convolution fusion | flops 4838129664 | bytes 20447232 | tf_op jit(solution)/shard_map/dot_general | solution.py:54
  96.7 0.5 reduce-scatter.5.cloned.1.call-update
  97.5 1.6 fusion.107
  99.4 7.7 %fusion.2 = f32[512,3072]{1,0:T(8,128)S(1)} fusion(bf16[1536,512]{0,1:T(8,128)(2,1)S(1)} %copy-done.6, bf16[1,2,3072,1536]{3,2,1,0:T(8,128)(2,1)} %param.11), kind=kOutput, calls=%fused_computation.2 | convolution fusion | flops 4831838208 | bytes 17301504 | tf_op jit(solution)/shard_map/dot_general | solution.py:54
  107.1 10.6 %fusion.16 = bf16[3072,512]{0,1:T(8,128)(2,1)} fusion(f32[512,3072]{1,0:T(8,128)S(1)} %fusion.2, bf16[1,2,3072,1536]{3,2,1,0:T(8,128)(2,1)} %param.11, bf16[1536,256]{0,1:T(8,128)(2,1)S(1)} %get-tuple-element.23, bf16[1536,256]{0,1:T(8,128)(2,1)S(1)} %get-tuple-element.22), kind=kOutput, calls=%fused_computation.19 | convolution fusion | flops 4838129664 | bytes 20447232 | tf_op jit(solution)/shard_map/dot_general | solution.py:54
  117.7 11.2 %all-gather.11.cloned.1.call-done = bf16[2,768,512]{2,1,0:T(8,128)(2,1)} async-done(((bf16[2,768,128]{2,1,0:T(8,128)(2,1)}), bf16[2,768,512]{2,1,0:T(8,128)(2,1)}) %all-gather.11.cloned.1.call-update) | async-done | bytes 1572880 | tf_op jit(solution)/shard_map/all_gather | solution.py:14
  128.9 3.7 %fusion.53 = f32[768,512]{0,1:T(8,128)S(1)} fusion(f32[1,2,512,512]{3,2,1,0:T(8,128)S(1)} %copy-done, f32[]{:T(128)} %bitcast.2, bf16[2,768,512]{2,1,0:T(8,128)(2,1)} %all-gather.11.cloned.1.call-done), kind=kOutput, calls=%fused_computation.60 | convolution fusion | flops 1209532416 | bytes 4194308 | tf_op jit(solution)/shard_map/dot_general | solution.py:10
  132.6 2.3 fusion.55
  134.9 1.6 add_convert_fusion
  136.6 2.5 subtract_convert_fusion.4
  139.1 52.8 %reduce-scatter.5.cloned.1.call-done = bf16[768,512]{0,1:T(8,128)(2,1)} async-done(((bf16[3072,512]{0,1:T(8,128)(2,1)}), bf16[768,512]{0,1:T(8,128)(2,1)}) %reduce-scatter.5.cloned.1.call-update) | async-done | bytes 786448 | tf_op jit(solution)/shard_map/reduce_scatter | solution.py:64
  191.9 2.5 fusion.105
  194.4 1.0 convolution_add_fusion
  195.6 58.8 %reduce-scatter.3.cloned.1.call-done = bf16[768,512]{0,1:T(8,128)(2,1)} async-done(((bf16[3072,512]{0,1:T(8,128)(2,1)}), bf16[768,512]{0,1:T(8,128)(2,1)}) %reduce-scatter.3.cloned.1.call-update) | async-done | bytes 786448 | tf_op jit(solution)/shard_map/reduce_scatter | solution.py:64
  254.4 2.8 fusion.106
  257.2 1.0 convolution_add_fusion.1
  258.3 1.1 pad_maximum_fusion.3
  259.4 1.1 pad_maximum_fusion.2
  260.5 0.6 copy-done.18
  261.2 0.6 fusion.111
  262.5 0.5 copy-done.1
  263.0 1.1 copy-done.2
  264.2 1.8 fusion.22
  266.0 5.7 %copy.13 = f32[1,768,2,512]{3,2,1,0:T(2,128)} copy(f32[1,768,2,512]{1,3,2,0:T(8,128)} %fusion.22) | data formatting | bytes 6291456
  271.7 4.3 %fusion.40 = bf16[768,1,512]{0,2,1:T(8,128)(2,1)} fusion(f32[768,2,256]{0,2,1:T(8,128)} %copy-done.2, f32[768,2,256]{0,2,1:T(8,128)} %copy-done.1, f32[]{:T(128)} %bitcast.24, f32[]{:T(128)} %bitcast.23), kind=kLoop, calls=%fused_computation.43 | loop fusion | flops 2359296 | bytes 3932168 | tf_op jit(solution)/shard_map/convert_element_type | solution.py:82
  276.0 4.2 %all-to-all-start = ((bf16[4,768,128]{1,2,0:T(8,128)(2,1)}), bf16[4,768,128]{1,2,0:T(8,128)(2,1)}, u32[]{:S(2)}, u32[]{:S(2)}) async-start(bf16[4,768,128]{1,2,0:T(8,128)(2,1)} %bitcast.26), calls=%async_computation.2 | async-start | bytes 1572864 | tf_op jit(solution)/shard_map/all_to_all | solution.py:84
  280.2 45.3 %all-reduce.3.cloned.1.call-done = (f32[2,512,256]{2,1,0:T(8,128)}, f32[2,512,256]{2,1,0:T(8,128)}) async-done(((f32[2,512,256]{2,1,0:T(8,128)}, f32[2,512,256]{2,1,0:T(8,128)}), (f32[2,512,256]{2,1,0:T(8,128)}, f32[2,512,256]{2,1,0:T(8,128)})) %all-reduce.3.cloned.1.call-update) | async-done | bytes 2097168 | tf_op jit(solution)/shard_map/psum | solution.py:76
  325.5 2.0 maximum_subtract_fusion.1
  327.5 2.4 fusion.60
  329.9 4.3 %all-to-all-start.1 = ((bf16[4,128,512]{2,1,0:T(8,128)(2,1)}), bf16[4,128,512]{2,1,0:T(8,128)(2,1)}, u32[]{:S(2)}, u32[]{:S(2)}) async-start(bf16[4,128,512]{2,1,0:T(8,128)(2,1)} %bitcast.94), calls=%async_computation.3 | async-start | bytes 1048576 | tf_op jit(solution)/shard_map/all_to_all | solution.py:89
  334.2 1.3 convert_reduce_fusion
  335.5 0.9 copy.14
  336.4 2.9 maximum_subtract_fusion
  339.3 2.2 all-to-all-done.1
  341.5 1.8 convert_reduce_fusion.1
  (56 shorter events, 2.1 us)
Async XLA Ops:
  7.2 47.4 %all-gather.5.cloned.1.call-start = ((), (), s32[]{:S(2)}) async-start(), calls=%async_computation.4 | async-start | bytes 1966080 | tf_op jit(solution)/shard_map/all_gather | solution.py:14
  8.3 49.6 %copy-start.8 = (bf16[2,768,128]{2,1,0:T(8,128)(2,1)}, bf16[2,768,128]{2,1,0:T(8,128)(2,1)S(1)}, u32[]{:S(2)}) copy-start(bf16[2,768,128]{2,1,0:T(8,128)(2,1)S(1)} %pad_maximum_fusion.6) | copy-start | bytes 1179652
  8.3 0.7 collective-permute-start
  9.0 0.7 copy-start.17
  9.8 66.6 %all-gather.9.cloned.1.call-start = ((), (), s32[]{:S(2)}) async-start(), calls=%async_computation.7 | async-start | bytes 2359296 | tf_op jit(solution)/shard_map/all_gather | solution.py:52
  54.6 3.2 copy-start
  57.9 2.9 copy-start.4
  66.4 31.1 %all-gather.7.cloned.1.call-start = ((), (), s32[]{:S(2)}) async-start(), calls=%async_computation.5 | async-start | bytes 2359296 | tf_op jit(solution)/shard_map/all_gather | solution.py:52
  67.4 61.5 %all-gather.11.cloned.1.call-start = ((), (), s32[]{:S(2)}) async-start(), calls=%async_computation.9 | async-start | bytes 1966080 | tf_op jit(solution)/shard_map/all_gather | solution.py:14
  76.3 9.2 %copy-start.7 = (bf16[1536,512]{0,1:T(8,128)(2,1)S(1)}, bf16[1536,512]{0,1:T(8,128)(2,1)}, u32[]{:S(2)}) copy-start(bf16[1536,512]{0,1:T(8,128)(2,1)} %all-gather.9.cloned.1.call-done) | copy-start | bytes 4718596
  96.7 95.2 %reduce-scatter.5.cloned.1.call-start = ((), (), s32[]{:S(2)}) async-start(), calls=%async_computation.8 | async-start | bytes 3932160 | tf_op jit(solution)/shard_map/reduce_scatter | solution.py:64
  97.3 157.1 %reduce-scatter.3.cloned.1.call-start = ((), (), s32[]{:S(2)}) async-start(), calls=%async_computation.6 | async-start | bytes 3932160 | tf_op jit(solution)/shard_map/reduce_scatter | solution.py:64
  97.5 1.9 copy-start.6
  117.7 207.9 %all-reduce.3.cloned.1.call-start = ((), (), s32[]{:S(2)}) async-start(), calls=%async_computation.10 | async-start | bytes 4194304 | tf_op jit(solution)/shard_map/psum | solution.py:76
  128.9 3.8 %copy-start.3 = (bf16[2,768,512]{2,1,0:T(8,128)(2,1)S(1)}, bf16[2,768,512]{2,1,0:T(8,128)(2,1)}, u32[]{:S(2)}) copy-start(bf16[2,768,512]{2,1,0:T(8,128)(2,1)} %all-gather.11.cloned.1.call-done) | copy-start | bytes 4718596
  136.6 57.8 %copy-start.9 = (bf16[768,512]{0,1:T(8,128)(2,1)}, bf16[768,512]{0,1:T(8,128)(2,1)S(1)}, u32[]{:S(2)}) copy-start(bf16[768,512]{0,1:T(8,128)(2,1)S(1)} %add_convert_fusion) | copy-start | bytes 2359300
  191.9 2.5 copy-start.11
  191.9 2.5 copy-start.13
  254.4 2.8 copy-start.10
  254.4 2.8 copy-start.12
  254.4 2.8 copy-start.15
  260.5 0.7 copy-start.18
  260.5 1.2 copy-start.14
  261.2 1.2 copy-start.16
  261.9 1.1 copy-start.1
  263.0 1.1 copy-start.2
  276.0 53.9 %all-to-all-start = ((bf16[4,768,128]{1,2,0:T(8,128)(2,1)}), bf16[4,768,128]{1,2,0:T(8,128)(2,1)}, u32[]{:S(2)}, u32[]{:S(2)}) async-start(bf16[4,768,128]{1,2,0:T(8,128)(2,1)} %bitcast.26), calls=%async_computation.2 | async-start | bytes 1572864 | tf_op jit(solution)/shard_map/all_to_all | solution.py:84
  329.9 6.5 %copy-start.5 = (f32[2,512,256]{2,1,0:T(8,128)S(1)}, f32[2,512,256]{2,1,0:T(8,128)}, u32[]{:S(2)}) copy-start(f32[2,512,256]{2,1,0:T(8,128)} %get-tuple-element.16) | copy-start | bytes 3145732
  329.9 11.6 %all-to-all-start.1 = ((bf16[4,128,512]{2,1,0:T(8,128)(2,1)}), bf16[4,128,512]{2,1,0:T(8,128)(2,1)}, u32[]{:S(2)}, u32[]{:S(2)}) async-start(bf16[4,128,512]{2,1,0:T(8,128)(2,1)} %bitcast.94), calls=%async_computation.3 | async-start | bytes 1048576 | tf_op jit(solution)/shard_map/all_to_all | solution.py:89
Sparse Core Ops, SparseCore 0:
  10.4 44.1 all-gather.4
  66.5 9.7 all-gather.8
  77.9 10.9 all-gather.6
  96.8 32.0 all-gather.10
  131.6 60.2 reduce-scatter.4
  194.0 60.2 reduce-scatter.2
  260.7 64.8 all-reduce.2
where the time goes:
time: 351 us; the launch traced here: 350 us
  waiting for transfers between devices  223 us (64%)
  matrix products  66.5 us (19%)
  other arithmetic  23.8 us (7%)
  between operations  15.1 us (4%)
  local copies, waits for them, and re-layouts  12.5 us (4%)
  starting transfers between devices  9.61 us (3%)
    reduce_scatter x2, waiting for transfers between devices, body(): lax.psum_scatter(partials[h], 'col', scatter_dimension=0, tiled=True)  112 us
    all_gather x2, waiting for transfers between devices, gather_panel(): return lax.all_gather(pair, 'pole', axis=2, tiled=True)  54 us
    psum x1, waiting for transfers between devices, body(): updates.append(lax.psum(update, ('row', 'col')))  45.3 us
    dot_general x2, matrix products, body(): jnp.dot(block_imag, turned, preferred_element_type=jnp.float32)  21.5 us
    dot_general x8, matrix products, precise(): jnp.dot(left, right, precision=lax.Precision.HIGH, preferred_element_type...  20.8 us
    dot_general x2, matrix products, body(): jnp.dot(block_real, rows, preferred_element_type=jnp.float32)  16.9 us
    unnamed x40, local copies, waits for them, and re-layouts  10.5 us
    all_gather x2, waiting for transfers between devices, body(): rows = lax.all_gather(mine, 'row', axis=0, tiled=True)  8.9 us
  transfers between devices with their start and end apart: 10, of which 7 were waited for; matrix products, arithmetic and copies ran while one was open for 22% of the time, Pallas kernels for 0%

commit v1 on v0

--- a/solution.py
+++ b/solution.py
@@ -73,7 +73,7 @@
                 square[:width, part:] + square[width:, :part],
             ]
         )
-        updates.append(lax.psum(update, ("row", "col")))
+        updates.append(lax.psum(lax.psum(update, "col"), "row"))
         columns.append(column.reshape(column.shape[0], 2, part))
     column = jnp.concatenate(columns, axis=2)
     pivot = inverse - jnp.concatenate(updates, axis=2)

time: 351 us -> 399 us (1.14)
  waiting for transfers between devices: 223 us -> 272 us
    psum x1 -> x2, waiting for transfers between devices: 45.3 us -> 90.9 us  [body(): updates.append(lax.psum(lax.psum(update, 'col'), 'row'))]
  transfers between devices with their start and end apart: 10 -> 11, of which waited for: 7 -> 9; matrix products, arithmetic and copies ran while one was open for 22% -> 20% of each run, Pallas kernels for 0% -> 0%
where the time goes in v1:
time: 399 us; the launch traced here: 398 us
  waiting for transfers between devices  272 us (68%)
  matrix products  66.5 us (17%)
  other arithmetic  23.7 us (6%)
  between operations  15.2 us (4%)
  local copies, waits for them, and re-layouts  11.9 us (3%)
  starting transfers between devices  9.52 us (2%)
    reduce_scatter x2, waiting for transfers between devices, body(): lax.psum_scatter(partials[h], 'col', scatter_dimension=0, tiled=True)  112 us
    psum x2, waiting for transfers between devices, body(): updates.append(lax.psum(lax.psum(update, 'col'), 'row'))  90.9 us
    all_gather x2, waiting for transfers between devices, gather_panel(): return lax.all_gather(pair, 'pole', axis=2, tiled=True)  54 us
    dot_general x2, matrix products, body(): jnp.dot(block_imag, turned, preferred_element_type=jnp.float32)  21.5 us
    dot_general x8, matrix products, precise(): jnp.dot(left, right, precision=lax.Precision.HIGH, preferred_element_type...  20.8 us
    dot_general x2, matrix products, body(): jnp.dot(block_real, rows, preferred_element_type=jnp.float32)  16.9 us
    unnamed x40, local copies, waits for them, and re-layouts  9.91 us
    all_gather x2, waiting for transfers between devices, body(): rows = lax.all_gather(mine, 'row', axis=0, tiled=True)  8.9 us
  transfers between devices with their start and end apart: 11, of which 9 were waited for; matrix products, arithmetic and copies ran while one was open for 20% of the time, Pallas kernels for 0%

profile of v1, /device:TPU:0, one launch (start us, length us, event | category | flops | bytes accessed | tf_op | source)
XLA Modules:
  0.0 398.3 jit_solution(6540354583518662620)
XLA Ops:
  7.2 1.1 pad_maximum_fusion.6
  8.3 0.7 collective-permute-start
  9.0 0.7 copy-done.17
  9.8 1.3 fusion.112
  11.8 42.8 %all-gather.5.cloned.1.call-done = bf16[2,768,512]{2,1,0:T(8,128)(2,1)} async-done(((bf16[2,768,128]{2,1,0:T(8,128)(2,1)}), bf16[2,768,512]{2,1,0:T(8,128)(2,1)}) %all-gather.5.cloned.1.call-update) | async-done | bytes 1572880 | tf_op jit(solution)/shard_map/all_gather | solution.py:14
  54.6 3.2 fusion.28
  57.9 2.9 fusion.26
  60.7 2.3 subtract_convert_fusion.5
  63.0 2.3 add_convert_fusion.1
  65.4 0.9 pad_maximum_fusion.5
  66.4 1.0 pad_maximum_fusion.4
  67.5 8.9 %all-gather.9.cloned.1.call-done = bf16[1536,512]{0,1:T(8,128)(2,1)} async-done(((bf16[768,512]{0,1:T(8,128)(2,1)}), bf16[1536,512]{0,1:T(8,128)(2,1)}) %all-gather.9.cloned.1.call-update) | async-done | bytes 1572880 | tf_op jit(solution)/shard_map/all_gather | solution.py:52
  76.3 9.2 %fusion = f32[512,3072]{1,0:T(8,128)S(1)} fusion(bf16[1536,512]{0,1:T(8,128)(2,1)} %all-gather.9.cloned.1.call-done, bf16[1,2,3072,1536]{3,2,1,0:T(8,128)(2,1)} %param.11), kind=kOutput, calls=%fused_computation | convolution fusion | flops 4831838208 | bytes 17301504 | tf_op jit(solution)/shard_map/dot_general | solution.py:54
  85.7 11.0 %fusion.19 = bf16[3072,512]{0,1:T(8,128)(2,1)} fusion(f32[512,3072]{1,0:T(8,128)S(1)} %fusion, bf16[1,2,3072,1536]{3,2,1,0:T(8,128)(2,1)} %param.11, bf16[1536,256]{0,1:T(8,128)(2,1)S(1)} %get-tuple-element.27, bf16[1536,256]{0,1:T(8,128)(2,1)S(1)} %get-tuple-element.26), kind=kOutput, calls=%fused_computation.20 | convolution fusion | flops 4838129664 | bytes 20447232 | tf_op jit(solution)/shard_map/dot_general | solution.py:54
  97.5 1.6 fusion.107
  99.4 7.7 %fusion.2 = f32[512,3072]{1,0:T(8,128)S(1)} fusion(bf16[1536,512]{0,1:T(8,128)(2,1)S(1)} %copy-done.6, bf16[1,2,3072,1536]{3,2,1,0:T(8,128)(2,1)} %param.11), kind=kOutput, calls=%fused_computation.2 | convolution fusion | flops 4831838208 | bytes 17301504 | tf_op jit(solution)/shard_map/dot_general | solution.py:54
  107.1 10.6 %fusion.16 = bf16[3072,512]{0,1:T(8,128)(2,1)} fusion(f32[512,3072]{1,0:T(8,128)S(1)} %fusion.2, bf16[1,2,3072,1536]{3,2,1,0:T(8,128)(2,1)} %param.11, bf16[1536,256]{0,1:T(8,128)(2,1)S(1)} %get-tuple-element.25, bf16[1536,256]{0,1:T(8,128)(2,1)S(1)} %get-tuple-element.24), kind=kOutput, calls=%fused_computation.19 | convolution fusion | flops 4838129664 | bytes 20447232 | tf_op jit(solution)/shard_map/dot_general | solution.py:54
  117.7 11.2 %all-gather.11.cloned.1.call-done = bf16[2,768,512]{2,1,0:T(8,128)(2,1)} async-done(((bf16[2,768,128]{2,1,0:T(8,128)(2,1)}), bf16[2,768,512]{2,1,0:T(8,128)(2,1)}) %all-gather.11.cloned.1.call-update) | async-done | bytes 1572880 | tf_op jit(solution)/shard_map/all_gather | solution.py:14
  128.9 3.7 fusion.53
  132.6 2.3 fusion.55
  134.9 1.6 add_convert_fusion
  136.6 2.5 subtract_convert_fusion.4
  139.1 52.8 %reduce-scatter.5.cloned.1.call-done = bf16[768,512]{0,1:T(8,128)(2,1)} async-done(((bf16[3072,512]{0,1:T(8,128)(2,1)}), bf16[768,512]{0,1:T(8,128)(2,1)}) %reduce-scatter.5.cloned.1.call-update) | async-done | bytes 786448 | tf_op jit(solution)/shard_map/reduce_scatter | solution.py:64
  191.9 2.5 fusion.105
  194.4 1.0 convolution_add_fusion
  195.6 58.8 %reduce-scatter.3.cloned.1.call-done = bf16[768,512]{0,1:T(8,128)(2,1)} async-done(((bf16[3072,512]{0,1:T(8,128)(2,1)}), bf16[768,512]{0,1:T(8,128)(2,1)}) %reduce-scatter.3.cloned.1.call-update) | async-done | bytes 786448 | tf_op jit(solution)/shard_map/reduce_scatter | solution.py:64
  254.4 2.8 fusion.106
  257.2 1.0 convolution_add_fusion.1
  258.3 1.0 pad_maximum_fusion.3
  259.4 1.0 pad_maximum_fusion.2
  260.5 87.2 %all-reduce.5.cloned.1.call-done = (f32[2,512,256]{2,1,0:T(8,128)}, f32[2,512,256]{2,1,0:T(8,128)}) async-done(((f32[2,512,256]{2,1,0:T(8,128)}, f32[2,512,256]{2,1,0:T(8,128)}), (f32[2,512,256]{2,1,0:T(8,128)}, f32[2,512,256]{2,1,0:T(8,128)})) %all-reduce.5.cloned.1.call-update) | async-done | bytes 2097168 | tf_op jit(solution)/shard_map/psum | solution.py:76
  347.7 0.6 fusion.111
  349.0 0.6 copy-done.1
  349.6 1.1 copy-done.2
  350.7 1.8 fusion.22
  352.5 5.8 %copy.13 = f32[1,768,2,512]{3,2,1,0:T(2,128)} copy(f32[1,768,2,512]{1,3,2,0:T(8,128)} %fusion.22) | data formatting | bytes 6291456
  358.3 4.3 %fusion.40 = bf16[768,1,512]{0,2,1:T(8,128)(2,1)} fusion(f32[768,2,256]{0,2,1:T(8,128)} %copy-done.2, f32[768,2,256]{0,2,1:T(8,128)} %copy-done.1, f32[]{:T(128)} %bitcast.24, f32[]{:T(128)} %bitcast.23), kind=kLoop, calls=%fused_computation.43 | loop fusion | flops 2359296 | bytes 3932168 | tf_op jit(solution)/shard_map/convert_element_type | solution.py:82
  362.6 4.2 %all-to-all-start = ((bf16[4,768,128]{1,2,0:T(8,128)(2,1)}), bf16[4,768,128]{1,2,0:T(8,128)(2,1)}, u32[]{:S(2)}, u32[]{:S(2)}) async-start(bf16[4,768,128]{1,2,0:T(8,128)(2,1)} %bitcast.26), calls=%async_computation.2 | async-start | bytes 1572864 | tf_op jit(solution)/shard_map/all_to_all | solution.py:84
  366.8 3.7 all-reduce.7.cloned.1.call-done
  370.5 2.0 maximum_subtract_fusion.1
  372.4 2.4 fusion.60
  374.8 3.1 all-to-all-done
  377.9 4.1 %all-to-all-start.1 = ((bf16[4,128,512]{2,1,0:T(8,128)(2,1)}), bf16[4,128,512]{2,1,0:T(8,128)(2,1)}, u32[]{:S(2)}, u32[]{:S(2)}) async-start(bf16[4,128,512]{2,1,0:T(8,128)(2,1)} %bitcast.94), calls=%async_computation.3 | async-start | bytes 1048576 | tf_op jit(solution)/shard_map/all_to_all | solution.py:89
  382.1 1.3 convert_reduce_fusion
  383.3 0.9 copy.14
  384.3 2.9 maximum_subtract_fusion
  387.2 2.5 all-to-all-done.1
  389.6 1.8 convert_reduce_fusion.1
  (59 shorter events, 2.6 us)
Async XLA Ops:
  7.2 47.4 %all-gather.5.cloned.1.call-start = ((), (), s32[]{:S(2)}) async-start(), calls=%async_computation.4 | async-start | bytes 1966080 | tf_op jit(solution)/shard_map/all_gather | solution.py:14
  8.3 49.6 %copy-start.8 = (bf16[2,768,128]{2,1,0:T(8,128)(2,1)}, bf16[2,768,128]{2,1,0:T(8,128)(2,1)S(1)}, u32[]{:S(2)}) copy-start(bf16[2,768,128]{2,1,0:T(8,128)(2,1)S(1)} %pad_maximum_fusion.6) | copy-start | bytes 1179652
  8.3 0.7 collective-permute-start
  9.0 0.7 copy-start.17
  9.8 66.6 %all-gather.9.cloned.1.call-start = ((), (), s32[]{:S(2)}) async-start(), calls=%async_computation.7 | async-start | bytes 2359296 | tf_op jit(solution)/shard_map/all_gather | solution.py:52
  54.6 3.2 copy-start
  57.9 2.9 copy-start.4
  66.4 31.1 %all-gather.7.cloned.1.call-start = ((), (), s32[]{:S(2)}) async-start(), calls=%async_computation.5 | async-start | bytes 2359296 | tf_op jit(solution)/shard_map/all_gather | solution.py:52
  67.4 61.5 %all-gather.11.cloned.1.call-start = ((), (), s32[]{:S(2)}) async-start(), calls=%async_computation.9 | async-start | bytes 1966080 | tf_op jit(solution)/shard_map/all_gather | solution.py:14
  76.3 9.2 %copy-start.7 = (bf16[1536,512]{0,1:T(8,128)(2,1)S(1)}, bf16[1536,512]{0,1:T(8,128)(2,1)}, u32[]{:S(2)}) copy-start(bf16[1536,512]{0,1:T(8,128)(2,1)} %all-gather.9.cloned.1.call-done) | copy-start | bytes 4718596
  96.7 95.2 %reduce-scatter.5.cloned.1.call-start = ((), (), s32[]{:S(2)}) async-start(), calls=%async_computation.8 | async-start | bytes 3932160 | tf_op jit(solution)/shard_map/reduce_scatter | solution.py:64
  97.3 157.1 %reduce-scatter.3.cloned.1.call-start = ((), (), s32[]{:S(2)}) async-start(), calls=%async_computation.6 | async-start | bytes 3932160 | tf_op jit(solution)/shard_map/reduce_scatter | solution.py:64
  97.5 1.9 copy-start.6
  117.7 230.0 %all-reduce.5.cloned.1.call-start = ((), (), s32[]{:S(2)}) async-start(), calls=%async_computation.10 | async-start | bytes 4194304 | tf_op jit(solution)/shard_map/psum | solution.py:76
  128.9 3.8 copy-start.3
  136.6 57.8 %copy-start.9 = (bf16[768,512]{0,1:T(8,128)(2,1)}, bf16[768,512]{0,1:T(8,128)(2,1)S(1)}, u32[]{:S(2)}) copy-start(bf16[768,512]{0,1:T(8,128)(2,1)S(1)} %add_convert_fusion) | copy-start | bytes 2359300
  191.9 2.5 copy-start.11
  191.9 2.5 copy-start.13
  254.4 2.8 copy-start.10
  254.4 2.8 copy-start.12
  254.4 2.8 copy-start.15
  260.4 87.3 %copy-start.18 = (f32[1,2]{1,0:T(1,128)S(1)}, f32[1,2]{1,0:T(1,128)}, u32[]{:S(2)}) copy-start(f32[1,2]{1,0:T(1,128)} %param.9) | copy-start | bytes 28
  260.4 87.9 %copy-start.14 = (bf16[768,512]{0,1:T(8,128)(2,1)S(1)}, bf16[768,512]{0,1:T(8,128)(2,1)}, u32[]{:S(2)}) copy-start(bf16[768,512]{0,1:T(8,128)(2,1)} %reduce-scatter.5.cloned.1.call-done) | copy-start | bytes 2359300
  260.4 110.0 %all-reduce.7.cloned.1.call-start = ((), (), s32[]{:S(2)}) async-start(), calls=%async_computation.11 | async-start | bytes 4194304 | tf_op jit(solution)/shard_map/psum | solution.py:76
  347.7 1.1 copy-start.16
  348.4 1.1 copy-start.1
  349.6 1.1 copy-start.2
  362.6 15.3 %all-to-all-start = ((bf16[4,768,128]{1,2,0:T(8,128)(2,1)}), bf16[4,768,128]{1,2,0:T(8,128)(2,1)}, u32[]{:S(2)}, u32[]{:S(2)}) async-start(bf16[4,768,128]{1,2,0:T(8,128)(2,1)} %bitcast.26), calls=%async_computation.2 | async-start | bytes 1572864 | tf_op jit(solution)/shard_map/all_to_all | solution.py:84
  374.8 9.4 %copy-start.5 = (f32[2,512,256]{2,1,0:T(8,128)S(1)}, f32[2,512,256]{2,1,0:T(8,128)}, u32[]{:S(2)}) copy-start(f32[2,512,256]{2,1,0:T(8,128)} %get-tuple-element.18) | copy-start | bytes 3145732
  377.9 11.7 %all-to-all-start.1 = ((bf16[4,128,512]{2,1,0:T(8,128)(2,1)}), bf16[4,128,512]{2,1,0:T(8,128)(2,1)}, u32[]{:S(2)}, u32[]{:S(2)}) async-start(bf16[4,128,512]{2,1,0:T(8,128)(2,1)} %bitcast.94), calls=%async_computation.3 | async-start | bytes 1048576 | tf_op jit(solution)/shard_map/all_to_all | solution.py:89
Sparse Core Ops, SparseCore 0:
  10.4 44.1 all-gather.4
  66.5 9.7 all-gather.8
  77.9 10.9 all-gather.6
  96.8 32.0 all-gather.10
  131.6 60.2 reduce-scatter.4
  194.0 60.2 reduce-scatter.2
  260.5 87.0 all-reduce.4
  350.2 20.2 all-reduce.6
